TPU v7x, 32 devices: a whole 2x2x4 slice. The times are simulated.
32 devices in a mesh: groups: 2 (over y), row: 4 (over x, core), col: 4 (over z).
Axes of the slice: x: 2, y: 2, z: 4, core: 2. Of those that a mesh axis runs over, the one named last changes fastest.
Arguments:
- adjacency: bfloat16 [8, 4, 32, 128, 128], P(('groups', 'row'), 'col'), parts along dimension 0, may hold values from 0.049804688 to 1
- tile_row: int32 [8, 4, 32], P(('groups', 'row'), 'col'), parts along dimension 0, may hold values from -1 to 7, as said below
- tile_col: int32 [8, 4, 32], P(('groups', 'row'), 'col'), parts along dimension 0, may hold values from -1 to 7, as said below
- seed_node: int32 [512], P('groups'), parts along dimension 0, may hold values from 0 to 4095
- teleport_block: int32 [512], P('groups'), parts along dimension 0, may hold values from 0 to 31
- previous: float32 [8192, 256], P(('groups', 'row', 'col')), parts along dimension 0, may hold values from 0.1 to 10
Outputs:
- rank_field: float32 [8192, 256], P(('groups', 'row', 'col')), parts along dimension 0
There are 2 independent parts, one for each index of `groups`. A program takes and returns all parts, laid end to end along the dimension named above; each array names one. Nothing has to cross between parts.
Inputs may be any that keep to these rules, and one draw needn't show every extreme that they name: On each device the slots with entries >= 0 come first, and tile_row and tile_col are -1 together on the other slots; a device's (tile_row, tile_col) pairs are distinct; in every part exactly one device has all 32 slots used and every other device uses between 5 and 10 of them. `tile_col`: empty exactly where tile_row is empty. In every part, for each index of row, at least one tile column holds no tile on any device with that index of row.
All inputs are finite; a program needn't handle non-finite values.
Results may differ from a plain program's by a relative error of at most 0.0003.
Values may be sent and summed in bfloat16 or wider, within the bound.
A program may use at most 64 MiB of HBM per device.

v0:
```python
import jax
import jax.numpy as jnp
from jax import lax
from jax.sharding import PartitionSpec as P

TILE = 128
ITERS = 3
damping = 0.85
highest = lax.Precision.HIGHEST


def teleport_weights(node_ids, seed_node, teleport_block):
    at_seed = (node_ids[:, None] == seed_node[None, :]).astype(jnp.float32)
    in_block = ((node_ids // TILE)[:, None] == teleport_block[None, :]).astype(jnp.float32)
    return 4.0 * at_seed + 2.0 * in_block


def block_sum(
    tile_stack, row_ids, col_ids, ordering, sorted_keys, rank_panel, first_row, block_rows
):
    slot_total = tile_stack.shape[0]
    tile_edge = tile_stack.shape[1]
    seed_width = rank_panel.shape[2]
    slot_batch = min(8, slot_total)
    first_live = jnp.sum((sorted_keys < first_row).astype(jnp.int32))
    past_live = jnp.sum((sorted_keys < first_row + block_rows).astype(jnp.int32))
    batches = (past_live - first_live + slot_batch - 1) // slot_batch

    def one_batch(batch_index, accumulated):
        for offset in range(slot_batch):
            position = first_live + batch_index * slot_batch + offset
            slot_index = lax.dynamic_index_in_dim(
                ordering, jnp.minimum(position, slot_total - 1), 0, keepdims=False
            )
            is_live = position < past_live
            target_row = lax.dynamic_index_in_dim(row_ids, slot_index, 0, keepdims=False)
            source_col = lax.dynamic_index_in_dim(col_ids, slot_index, 0, keepdims=False)
            target = jnp.clip(target_row - first_row, 0, block_rows - 1)
            source = jnp.maximum(source_col, 0)
            one_tile = lax.dynamic_index_in_dim(tile_stack, slot_index, 0, keepdims=False)
            panel_block = lax.dynamic_index_in_dim(rank_panel, source, 0, keepdims=False)
            product = jnp.dot(one_tile, panel_block, preferred_element_type=jnp.float32)
            current = lax.dynamic_index_in_dim(accumulated, target, 0, keepdims=False)
            updated = current + jnp.where(is_live, product, jnp.zeros_like(product))
            accumulated = lax.dynamic_update_index_in_dim(accumulated, updated, target, 0)
        return accumulated

    start_sum = jnp.zeros((block_rows, tile_edge, seed_width), jnp.float32)
    result = lax.fori_loop(0, batches, one_batch, start_sum)
    return result.reshape(block_rows * tile_edge, seed_width)


def on_device(adjacency, tile_row, tile_col, seed_node, teleport_block, previous):
    tile_stack = adjacency[0, 0]
    row_ids = tile_row[0, 0]
    col_ids = tile_col[0, 0]
    owned_rows, seed_width = previous.shape
    slot_total = tile_stack.shape[0]
    tile_edge = tile_stack.shape[1]
    row_devices = lax.axis_size("row")
    col_devices = lax.axis_size("col")
    tile_rows = owned_rows * row_devices // tile_edge
    tile_cols = owned_rows * col_devices // tile_edge
    sort_keys = jnp.where(row_ids >= 0, row_ids, tile_rows)
    slot_order = jnp.arange(slot_total, dtype=jnp.int32)
    sorted_keys, ordering = lax.sort((sort_keys, slot_order), num_keys=1, is_stable=True)
    col_place = (col_ids[:, None] == jnp.arange(tile_cols, dtype=jnp.int32)[None, :]).astype(
        jnp.float32
    )
    tile_sums = jnp.sum(tile_stack.astype(jnp.float32), axis=1)
    col_sums = jnp.einsum("tj,tb->jb", col_place, tile_sums, precision=highest).reshape(
        tile_cols * tile_edge
    )
    full_divisor = jnp.maximum(lax.psum(col_sums, "col"), 1.0)
    first_node = (lax.axis_index("row") * col_devices + lax.axis_index("col")) * owned_rows
    node_ids = first_node + jnp.arange(owned_rows, dtype=jnp.int32)
    teleport = teleport_weights(node_ids, seed_node, teleport_block)
    rank_field = previous
    for iteration in range(ITERS):
        gathered = lax.all_gather(rank_field, "col", axis=0, tiled=True)
        rank_panel = (gathered / full_divisor[:, None]).astype(jnp.bfloat16)
        rank_panel = rank_panel.reshape(tile_cols, tile_edge, seed_width)
        partial_sum = block_sum(
            tile_stack, row_ids, col_ids, ordering, sorted_keys, rank_panel, 0, tile_rows
        )
        summed = lax.psum_scatter(partial_sum, "row", scatter_dimension=0, tiled=True)
        rank_field = damping * summed + (1.0 - damping) * teleport
    return rank_field


def solution(mesh):
    in_specs = (
        P(("groups", "row"), "col", None, None, None),
        P(("groups", "row"), "col", None),
        P(("groups", "row"), "col", None),
        P("groups"),
        P("groups"),
        P(("groups", "row", "col"), None),
    )
    out_specs = P(("groups", "row", "col"), None)
    return jax.shard_map(
        on_device, mesh=mesh, in_specs=in_specs, out_specs=out_specs, check_vma=False
    )
```

profile of v0, /device:TPU:0, one launch (start us, length us, event | category | flops | bytes accessed | tf_op | source)
XLA Modules:
  0.0 590.8 jit_solution(7642503846385073427)
XLA Ops:
  6.5 0.7 all-gather.4.cloned.1.call-update
  7.3 0.7 compare_select_fusion
  8.0 1.1 sort.15
  9.0 0.7 fusion.195
  11.1 1.4 convert_reduce_fusion
  12.5 0.3 convolution_bitcast_fusion
  12.7 13.6 %psum.7 = f32[1024]{0:T(1024)S(1)} all-reduce(f32[1024]{0:T(1024)S(1)} %convolution_bitcast_fusion), channel_id=1, replica_groups=mesh['groups'=2,'row'=4,'col'=4] {'col'}, use_global_device_ids=true, to_apply=%region_4.5 | all-reduce | flops 1024 | bytes 8192 | tf_op jit(solution)/shard_map/psum | solution.py:74
  26.4 13.3 %all-gather.4.cloned.1.call-done = f32[1024,256]{1,0:T(8,128)} async-done(((f32[256,256]{1,0:T(8,128)}), f32[1024,256]{1,0:T(8,128)}) %all-gather.4.cloned.1.call-update) | async-done | bytes 1048592 | tf_op jit(solution)/shard_map/all_gather | solution.py:80
  39.6 1.4 divide_convert_fusion.2
  41.2 33.7 %while.30 = (s32[]{:T(128)}, f32[8,128,256]{2,1,0:T(8,128)S(1)}, s32[]{:T(128)}, s32[]{:T(128)}, s32[32]{0:T(128)S(1)}, /*index=5*/s32[32]{0:T(128)S(1)}, s32[]{...) while((s32[]{:T(128)}, f32[8,128,256]{2,1,0:T(8,128)S(1)}, ...), condition=%wide.region_6.7_spmd, body=%wide.region_5.6_spmd.sunk | while | flops 67633232 | bytes 4982441 | solution.py:49
  41.9 0.7 fusion.300
  57.6 0.7 fusion.301
  60.3 0.2 fusion.302
  62.3 0.2 fusion.303
  64.5 0.2 fusion.304
  66.5 0.2 fusion.305
  70.5 0.2 fusion.307
  72.6 0.2 fusion.308
  74.7 0.2 fusion.309
  74.9 0.9 copy-done.1
  76.0 124.4 %reduce-scatter.4.cloned.1.call-done = f32[256,256]{1,0:T(8,128)} async-done(((f32[1024,256]{1,0:T(8,128)}), f32[256,256]{1,0:T(8,128)}) %reduce-scatter.4.cloned.1.call-update) | async-done | bytes 262160 | tf_op jit(solution)/shard_map/reduce_scatter | solution.py:86
  200.4 1.8 fusion.192
  202.2 28.1 %all-gather.6.cloned.1.call-done = f32[1024,256]{1,0:T(8,128)} async-done(((f32[256,256]{1,0:T(8,128)}), f32[1024,256]{1,0:T(8,128)}) %all-gather.6.cloned.1.call-update) | async-done | bytes 1048592 | tf_op jit(solution)/shard_map/all_gather | solution.py:80
  230.3 1.4 divide_convert_fusion.1
  231.8 33.8 %while.31 = (s32[]{:T(128)}, f32[8,128,256]{2,1,0:T(8,128)S(1)}, s32[]{:T(128)}, s32[]{:T(128)}, s32[32]{0:T(128)S(1)}, /*index=5*/s32[32]{0:T(128)S(1)}, s32[]{...) while((s32[]{:T(128)}, f32[8,128,256]{2,1,0:T(8,128)S(1)}, ...), condition=%wide.region_9.10_spmd, body=%wide.region_8.9_spmd.sunk | while | flops 67633232 | bytes 4982441 | solution.py:49
  232.5 0.7 fusion.326
  248.3 0.7 fusion.327
  251.0 0.2 fusion.328
  257.2 0.2 fusion.331
  261.2 0.2 fusion.333
  263.3 0.2 fusion.334
  265.5 0.2 fusion.335
  265.7 1.0 copy-done.2
  266.7 124.6 %reduce-scatter.6.cloned.1.call-done = f32[256,256]{1,0:T(8,128)} async-done(((f32[1024,256]{1,0:T(8,128)}), f32[256,256]{1,0:T(8,128)}) %reduce-scatter.6.cloned.1.call-update) | async-done | bytes 262160 | tf_op jit(solution)/shard_map/reduce_scatter | solution.py:86
  391.3 1.8 multiply_add_fusion.1
  393.2 28.0 %all-gather.8.cloned.1.call-done = f32[1024,256]{1,0:T(8,128)} async-done(((f32[256,256]{1,0:T(8,128)}), f32[1024,256]{1,0:T(8,128)}) %all-gather.8.cloned.1.call-update) | async-done | bytes 1048592 | tf_op jit(solution)/shard_map/all_gather | solution.py:80
  421.2 1.4 divide_convert_fusion
  422.7 33.8 %while.32 = (s32[]{:T(128)}, f32[8,128,256]{2,1,0:T(8,128)S(1)}, s32[]{:T(128)}, s32[]{:T(128)}, s32[32]{0:T(128)S(1)}, /*index=5*/s32[32]{0:T(128)S(1)}, s32[]{...) while((s32[]{:T(128)}, f32[8,128,256]{2,1,0:T(8,128)S(1)}, ...), condition=%wide.region_12.13_spmd, body=%wide.region_11.12_spmd.sunk | while | flops 67633232 | bytes 4982441 | solution.py:49
  423.5 0.7 fusion.352
  439.2 0.7 fusion.353
  441.9 0.2 fusion.354
  446.0 0.2 fusion.356
  448.1 0.2 fusion.357
  452.2 0.2 fusion.359
  456.4 0.2 fusion.361
  456.6 1.0 copy-done
  457.5 124.6 %reduce-scatter.8.cloned.1.call-done = f32[256,256]{1,0:T(8,128)} async-done(((f32[1024,256]{1,0:T(8,128)}), f32[256,256]{1,0:T(8,128)}) %reduce-scatter.8.cloned.1.call-update) | async-done | bytes 262160 | tf_op jit(solution)/shard_map/reduce_scatter | solution.py:86
  582.2 1.8 multiply_add_fusion
  (61 shorter events, 2.1 us)
Async XLA Ops:
  6.5 5.9 %copy-start.5 = (s32[1,1,32]{2,1,0:T(1,128)S(1)}, s32[1,1,32]{2,1,0:T(1,128)}, u32[]{:S(2)}) copy-start(s32[1,1,32]{2,1,0:T(1,128)} %param.14) | copy-start | bytes 388
  6.5 33.1 %all-gather.4.cloned.1.call-start = ((), (), s32[]{:S(2)}) async-start(), calls=%async_computation.3 | async-start | bytes 1310720 | tf_op jit(solution)/shard_map/all_gather | solution.py:80
  7.3 193.1 %reduce-scatter.4.cloned.1.call-start = ((), (), s32[]{:S(2)}) async-start(), calls=%async_computation.4 | async-start | bytes 1310720 | tf_op jit(solution)/shard_map/reduce_scatter | solution.py:86
  26.4 14.8 %copy-start.3 = (bf16[1,1,32,128,128]{4,3,2,1,0:T(8,128)(2,1)S(1)}, bf16[1,1,32,128,128]{4,3,2,1,0:T(8,128)(2,1)}, u32[]{:S(2)}) copy-start(bf16[1,1,32,128,128]{4,3,2,1,0:T(8,128)(2,1)} %param.12) | copy-start | bytes 3145732
  26.4 14.8 %copy-start.4 = (s32[1,1,32]{2,1,0:T(1,128)S(1)}, s32[1,1,32]{2,1,0:T(1,128)}, u32[]{:S(2)}) copy-start(s32[1,1,32]{2,1,0:T(1,128)} %param.13) | copy-start | bytes 388
  74.9 1.0 copy-start.1
  74.9 125.5 %copy-start.6 = (s32[256]{0:T(256)S(1)}, s32[256]{0:T(256)}, u32[]{:S(2)}) copy-start(s32[256]{0:T(256)} %param.16) | copy-start | bytes 3076
  74.9 125.4 %copy-start.7 = (s32[256]{0:T(256)S(1)}, s32[256]{0:T(256)}, u32[]{:S(2)}) copy-start(s32[256]{0:T(256)} %param.15) | copy-start | bytes 3076
  75.9 154.4 %all-gather.6.cloned.1.call-start = ((), (), s32[]{:S(2)}) async-start(), calls=%async_computation.5 | async-start | bytes 1310720 | tf_op jit(solution)/shard_map/all_gather | solution.py:80
  202.2 189.1 %reduce-scatter.6.cloned.1.call-start = ((), (), s32[]{:S(2)}) async-start(), calls=%async_computation.6 | async-start | bytes 1310720 | tf_op jit(solution)/shard_map/reduce_scatter | solution.py:86
  265.6 1.0 copy-start.2
  266.6 154.6 %all-gather.8.cloned.1.call-start = ((), (), s32[]{:S(2)}) async-start(), calls=%async_computation.7 | async-start | bytes 1310720 | tf_op jit(solution)/shard_map/all_gather | solution.py:80
  393.1 189.1 %reduce-scatter.8.cloned.1.call-start = ((), (), s32[]{:S(2)}) async-start(), calls=%async_computation.8 | async-start | bytes 1310720 | tf_op jit(solution)/shard_map/reduce_scatter | solution.py:86
  456.5 1.0 copy-start
Sparse Core Ops, SparseCore 0:
  8.9 30.6 all-gather.3
  76.0 124.3 reduce-scatter.3
  202.3 27.9 all-gather.5
  266.8 124.4 reduce-scatter.5
  393.2 27.9 all-gather.7
  457.7 124.4 reduce-scatter.7
where the time goes:
time: 596 us; the launch traced here: 591 us
  waiting for transfers between devices  444 us (74%)
  loops' own time  92.9 us (16%)
  between operations  14.9 us (2%)
  other arithmetic  13.6 us (2%)
  blocking collectives  13.6 us (2%)
  local copies, waits for them, and re-layouts  7.78 us (1%)
    reduce_scatter x3, waiting for transfers between devices, on_device(): lax.psum_scatter(partial_sum, 'row', scatter_dimension=0, tiled=True)  374 us
    another operation x3, loops' own time, block_sum(): result = lax.fori_loop(0, batches, one_batch, start_sum)  92.9 us
    all_gather x3, waiting for transfers between devices, on_device(): gathered = lax.all_gather(rank_field, 'col', axis=0, tiled=True)  69.4 us
    psum x1, blocking collectives, on_device(): full_divisor = jnp.maximum(lax.psum(col_sums, 'col'), 1.0)  13.6 us
  transfers between devices with their start and end apart: 6, of which 6 were waited for; matrix products, arithmetic and copies ran while one was open for 1% of the time, Pallas kernels for 0%

commit v1 on v0

--- a/solution.py
+++ b/solution.py
@@ -77,7 +77,26 @@
     teleport = teleport_weights(node_ids, seed_node, teleport_block)
     rank_field = previous
     for iteration in range(ITERS):
-        gathered = lax.all_gather(rank_field, "col", axis=0, tiled=True)
+        length, index, rows = (lax.axis_size("col"), lax.axis_index("col"), rank_field.shape[0])
+        right = [(i, (i + 1) % length) for i in range(length)]
+        behind = [(i, (i - 1) % length) for i in range(length)]
+        whole = jnp.zeros(
+            (*rank_field.shape[:0], length * rows, *rank_field.shape[0 + 1 :]), rank_field.dtype
+        )
+        whole = lax.dynamic_update_slice_in_dim(whole, rank_field, index * rows, axis=0)
+        from_left = from_right = rank_field
+        middle = length // 2
+        for turn in range(1, middle + 1):
+            from_left = lax.ppermute(from_left, "col", right)
+            whole = lax.dynamic_update_slice_in_dim(
+                whole, from_left, (index - turn) % length * rows, axis=0
+            )
+            if turn < length - middle:
+                from_right = lax.ppermute(from_right, "col", behind)
+                whole = lax.dynamic_update_slice_in_dim(
+                    whole, from_right, (index + turn) % length * rows, axis=0
+                )
+        gathered = whole
         rank_panel = (gathered / full_divisor[:, None]).astype(jnp.bfloat16)
         rank_panel = rank_panel.reshape(tile_cols, tile_edge, seed_width)
         partial_sum = block_sum(

time: 596 us -> 559 us (0.938)
  waiting for transfers between devices: 444 us -> 401 us
  starting transfers between devices: 0.21 us -> 13.3 us
  other arithmetic: 13.6 us -> 5.86 us
    all_gather x3 -> x0, waiting for transfers between devices: 69.4 us -> none  [on_device(): gathered = lax.all_gather(rank_field, 'col', axis=0, tiled=True)]
    ppermute x0 -> x9, waiting for transfers between devices: none -> 40.5 us  [the longest x6 31.9 us: on_device(): from_left = lax.ppermute(from_left, 'col', right)]
    ppermute x0 -> x9, starting transfers between devices: none -> 13.2 us  [the longest x3 6.73 us: on_device(): from_right = lax.ppermute(from_right, 'col', behind)]
    reduce_scatter x3, waiting for transfers between devices: 374 us -> 361 us  [on_device(): lax.psum_scatter(partial_sum, 'row', scatter_dimension=0, tiled=True)]
  transfers between devices with their start and end apart: 6 -> 12, of which waited for: 6 -> 10; matrix products, arithmetic and copies ran while one was open for 1% -> 1% of each run, Pallas kernels for 0% -> 0%
where the time goes in v1:
time: 559 us; the launch traced here: 554 us
  waiting for transfers between devices  401 us (72%)
  loops' own time  90.4 us (16%)
  between operations  14.6 us (3%)
  blocking collectives  13.9 us (2%)
  starting transfers between devices  13.3 us (2%)
  local copies, waits for them, and re-layouts  10.9 us (2%)
  other arithmetic  5.86 us (1%)
    reduce_scatter x3, waiting for transfers between devices, on_device(): lax.psum_scatter(partial_sum, 'row', scatter_dimension=0, tiled=True)  361 us
    another operation x3, loops' own time, block_sum(): result = lax.fori_loop(0, batches, one_batch, start_sum)  90.4 us
    ppermute x6, waiting for transfers between devices, on_device(): from_left = lax.ppermute(from_left, 'col', right)  31.9 us
    psum x1, blocking collectives, on_device(): full_divisor = jnp.maximum(lax.psum(col_sums, 'col'), 1.0)  13.9 us
  transfers between devices with their start and end apart: 12, of which 10 were waited for; matrix products, arithmetic and copies ran while one was open for 1% of the time, Pallas kernels for 0%

profile of v1, /device:TPU:0, one launch (start us, length us, event | category | flops | bytes accessed | tf_op | source)
XLA Modules:
  0.0 554.1 jit_solution(12755256588937974636)
XLA Ops:
  6.5 3.0 collective-permute-start
  9.6 2.1 collective-permute-start.1
  11.7 1.5 convert_reduce_fusion
  13.1 0.2 convolution_bitcast_fusion
  13.4 13.9 %psum.7 = f32[1024]{0:T(1024)S(1)} all-reduce(f32[1024]{0:T(1024)S(1)} %convolution_bitcast_fusion), channel_id=1, replica_groups=mesh['groups'=2,'row'=4,'col'=4] {'col'}, use_global_device_ids=true, to_apply=%region_4.5 | all-reduce | flops 1024 | bytes 8192 | tf_op jit(solution)/shard_map/psum | solution.py:74
  27.4 1.1 sort.15
  28.5 0.3 collective-permute-start.2
  28.8 0.6 fusion.195
  30.7 6.0 %collective-permute-done.2 = f32[256,256]{1,0:T(8,128)S(1)} collective-permute-done((f32[256,256]{1,0:T(8,128)S(1)}, f32[256,256]{1,0:T(8,128)S(1)}, u32[]{:S(2)}, u32[]{:S(2)}) %collective-permute-start.2) | collective-permute-done | bytes 262176 | tf_op jit(solution)/shard_map/ppermute | solution.py:90
  36.8 0.2 divide_convert_fusion.2
  37.1 0.9 copy-done.3
  38.0 33.0 %while.30 = (s32[]{:T(128)}, f32[8,128,256]{2,1,0:T(8,128)S(1)}, s32[]{:T(128)}, s32[]{:T(128)}, s32[32]{0:T(128)S(1)}, /*index=5*/s32[32]{0:T(128)S(1)}, s32[]{...) while((s32[]{:T(128)}, f32[8,128,256]{2,1,0:T(8,128)S(1)}, ...), condition=%wide.region_6.7_spmd, body=%wide.region_5.6_spmd.sunk | while | flops 67633232 | bytes 4982441 | solution.py:49
  38.6 0.7 fusion.301
  54.1 0.7 fusion.302
  60.8 0.2 fusion.305
  62.8 0.2 fusion.306
  71.0 0.9 copy-done.1
  72.0 117.1 %reduce-scatter.4.cloned.1.call-done = f32[256,256]{1,0:T(8,128)} async-done(((f32[1024,256]{1,0:T(8,128)}), f32[256,256]{1,0:T(8,128)}) %reduce-scatter.4.cloned.1.call-update) | async-done | bytes 262160 | tf_op jit(solution)/shard_map/reduce_scatter | solution.py:105
  189.2 0.9 copy-done.7
  190.2 1.6 collective-permute-start.3
  191.8 2.3 collective-permute-start.4
  194.1 7.2 %collective-permute-done.3 = f32[256,256]{1,0:T(8,128)S(1)} collective-permute-done((f32[256,256]{1,0:T(8,128)S(1)}, f32[256,256]{1,0:T(8,128)S(1)}, u32[]{:S(2)}, u32[]{:S(2)}) %collective-permute-start.3) | collective-permute-done | bytes 262176 | tf_op jit(solution)/shard_map/ppermute | solution.py:90
  201.3 4.3 collective-permute-done.4
  205.7 5.7 %collective-permute-done.5 = f32[256,256]{1,0:T(8,128)S(1)} collective-permute-done((f32[256,256]{1,0:T(8,128)S(1)}, f32[256,256]{1,0:T(8,128)S(1)}, u32[]{:S(2)}, u32[]{:S(2)}) %collective-permute-start.5) | collective-permute-done | bytes 262176 | tf_op jit(solution)/shard_map/ppermute | solution.py:90
  211.4 0.2 divide_convert_fusion.1
  211.7 33.0 %while.31 = (s32[]{:T(128)}, f32[8,128,256]{2,1,0:T(8,128)S(1)}, s32[]{:T(128)}, s32[]{:T(128)}, s32[32]{0:T(128)S(1)}, /*index=5*/s32[32]{0:T(128)S(1)}, s32[]{...) while((s32[]{:T(128)}, f32[8,128,256]{2,1,0:T(8,128)S(1)}, ...), condition=%wide.region_9.10_spmd, body=%wide.region_8.9_spmd.sunk | while | flops 67633232 | bytes 4982441 | solution.py:49
  212.4 0.7 fusion.327
  227.9 0.7 fusion.328
  234.6 0.2 fusion.331
  236.6 0.2 fusion.332
  242.6 0.2 fusion.335
  244.7 1.0 copy-done.2
  245.8 121.7 %reduce-scatter.6.cloned.1.call-done = f32[256,256]{1,0:T(8,128)} async-done(((f32[1024,256]{1,0:T(8,128)}), f32[256,256]{1,0:T(8,128)}) %reduce-scatter.6.cloned.1.call-update) | async-done | bytes 262160 | tf_op jit(solution)/shard_map/reduce_scatter | solution.py:105
  367.5 0.9 copy-done.8
  368.5 1.5 collective-permute-start.6
  370.1 2.3 collective-permute-start.7
  372.4 7.2 %collective-permute-done.6 = f32[256,256]{1,0:T(8,128)S(1)} collective-permute-done((f32[256,256]{1,0:T(8,128)S(1)}, f32[256,256]{1,0:T(8,128)S(1)}, u32[]{:S(2)}, u32[]{:S(2)}) %collective-permute-start.6) | collective-permute-done | bytes 262176 | tf_op jit(solution)/shard_map/ppermute | solution.py:90
  379.7 4.3 collective-permute-done.7
  384.0 5.7 %collective-permute-done.8 = f32[256,256]{1,0:T(8,128)S(1)} collective-permute-done((f32[256,256]{1,0:T(8,128)S(1)}, f32[256,256]{1,0:T(8,128)S(1)}, u32[]{:S(2)}, u32[]{:S(2)}) %collective-permute-start.8) | collective-permute-done | bytes 262176 | tf_op jit(solution)/shard_map/ppermute | solution.py:90
  389.7 0.2 divide_convert_fusion
  390.1 33.0 %while.32 = (s32[]{:T(128)}, f32[8,128,256]{2,1,0:T(8,128)S(1)}, s32[]{:T(128)}, s32[]{:T(128)}, s32[32]{0:T(128)S(1)}, /*index=5*/s32[32]{0:T(128)S(1)}, s32[]{...) while((s32[]{:T(128)}, f32[8,128,256]{2,1,0:T(8,128)S(1)}, ...), condition=%wide.region_12.13_spmd, body=%wide.region_11.12_spmd.sunk | while | flops 67633232 | bytes 4982441 | solution.py:49
  390.7 0.7 fusion.353
  406.2 0.7 fusion.354
  412.9 0.2 fusion.357
  414.9 0.2 fusion.358
  423.0 1.0 copy-done
  424.0 121.7 %reduce-scatter.8.cloned.1.call-done = f32[256,256]{1,0:T(8,128)} async-done(((f32[1024,256]{1,0:T(8,128)}), f32[256,256]{1,0:T(8,128)}) %reduce-scatter.8.cloned.1.call-update) | async-done | bytes 262160 | tf_op jit(solution)/shard_map/reduce_scatter | solution.py:105
  545.7 1.8 multiply_add_fusion
  (89 shorter events, 4.2 us)
Async XLA Ops:
  6.5 6.6 %copy-start.5 = (s32[1,1,32]{2,1,0:T(1,128)S(1)}, s32[1,1,32]{2,1,0:T(1,128)}, u32[]{:S(2)}) copy-start(s32[1,1,32]{2,1,0:T(1,128)} %param.14) | copy-start | bytes 388
  6.5 20.7 %copy-start.4 = (s32[1,1,32]{2,1,0:T(1,128)S(1)}, s32[1,1,32]{2,1,0:T(1,128)}, u32[]{:S(2)}) copy-start(s32[1,1,32]{2,1,0:T(1,128)} %param.13) | copy-start | bytes 388
  6.5 182.6 %reduce-scatter.4.cloned.1.call-start = ((), (), s32[]{:S(2)}) async-start(), calls=%async_computation.3 | async-start | bytes 1310720 | tf_op jit(solution)/shard_map/reduce_scatter | solution.py:105
  6.5 21.9 %collective-permute-start = (f32[256,256]{1,0:T(8,128)}, f32[256,256]{1,0:T(8,128)S(1)}, u32[]{:S(2)}, u32[]{:S(2)}) collective-permute-start(f32[256,256]{1,0:T(8,128)} %param.17), channel_id=1, source_target_pairs={{0,1},{1,2},{2,3},{3,0},{4,5},{5,6},{6,7},{7,4},{8,9},{9,10},{10,1... | collective-permute-start | bytes 786440 | tf_op jit(solution)/shard_map/ppermute | solution.py:90
  9.6 21.1 %collective-permute-start.1 = (f32[256,256]{1,0:T(8,128)}, f32[256,256]{1,0:T(8,128)S(1)}, u32[]{:S(2)}, u32[]{:S(2)}) collective-permute-start(f32[256,256]{1,0:T(8,128)} %param.17), channel_id=1, source_target_pairs={{0,3},{1,0},{2,1},{3,2},{4,7},{5,4},{6,5},{7,6},{8,11},{9,8},{10,9... | collective-permute-start | bytes 786440 | tf_op jit(solution)/shard_map/ppermute | solution.py:95
  11.6 15.7 %copy-start.6 = (f32[256,256]{1,0:T(8,128)S(1)}, f32[256,256]{1,0:T(8,128)}, u32[]{:S(2)}) copy-start(f32[256,256]{1,0:T(8,128)} %param.17) | copy-start | bytes 786436
  28.5 8.2 %collective-permute-start.2 = (f32[256,256]{1,0:T(8,128)S(1)}, f32[256,256]{1,0:T(8,128)S(1)}, u32[]{:S(2)}, u32[]{:S(2)}) collective-permute-start(f32[256,256]{1,0:T(8,128)S(1)} %collective-permute-done), channel_id=1, source_target_pairs={{0,1},{1,2},{2,3},{3,0},{4,5},{5,6},{6,7},{7,4},{8,9},{9,10},{10,1... | collective-permute-start | bytes 786440 | tf_op jit(solution)/shard_map/ppermute | solution.py:90
  36.7 1.2 copy-start.3
  70.9 1.0 copy-start.1
  70.9 118.3 %copy-start.9 = (s32[256]{0:T(256)S(1)}, s32[256]{0:T(256)}, u32[]{:S(2)}) copy-start(s32[256]{0:T(256)} %param.16) | copy-start | bytes 3076
  71.0 118.3 %copy-start.10 = (s32[256]{0:T(256)S(1)}, s32[256]{0:T(256)}, u32[]{:S(2)}) copy-start(s32[256]{0:T(256)} %param.15) | copy-start | bytes 3076
  71.9 295.5 %reduce-scatter.6.cloned.1.call-start = ((), (), s32[]{:S(2)}) async-start(), calls=%async_computation.4 | async-start | bytes 1310720 | tf_op jit(solution)/shard_map/reduce_scatter | solution.py:105
  189.1 0.9 copy-start.7
  190.2 11.1 %collective-permute-start.3 = (f32[256,256]{1,0:T(8,128)S(1)}, f32[256,256]{1,0:T(8,128)S(1)}, u32[]{:S(2)}, u32[]{:S(2)}) collective-permute-start(f32[256,256]{1,0:T(8,128)S(1)} %get-tuple-element.236), channel_id=1, source_target_pairs={{0,1},{1,2},{2,3},{3,0},{4,5},{5,6},{6,7},{7,4},{8,9},{9,10},{10,1... | collective-permute-start | bytes 786440 | tf_op jit(solution)/shard_map/ppermute | solution.py:90
  191.8 13.9 %collective-permute-start.4 = (f32[256,256]{1,0:T(8,128)S(1)}, f32[256,256]{1,0:T(8,128)S(1)}, u32[]{:S(2)}, u32[]{:S(2)}) collective-permute-start(f32[256,256]{1,0:T(8,128)S(1)} %get-tuple-element.236), channel_id=1, source_target_pairs={{0,3},{1,0},{2,1},{3,2},{4,7},{5,4},{6,5},{7,6},{8,11},{9,8},{10,9... | collective-permute-start | bytes 786440 | tf_op jit(solution)/shard_map/ppermute | solution.py:95
  201.3 10.1 %collective-permute-start.5 = (f32[256,256]{1,0:T(8,128)S(1)}, f32[256,256]{1,0:T(8,128)S(1)}, u32[]{:S(2)}, u32[]{:S(2)}) collective-permute-start(f32[256,256]{1,0:T(8,128)S(1)} %collective-permute-done.3), channel_id=1, source_target_pairs={{0,1},{1,2},{2,3},{3,0},{4,5},{5,6},{6,7},{7,4},{8,9},{9,10},{10,1... | collective-permute-start | bytes 786440 | tf_op jit(solution)/shard_map/ppermute | solution.py:90
  244.7 1.0 copy-start.2
  245.7 300.0 %reduce-scatter.8.cloned.1.call-start = ((), (), s32[]{:S(2)}) async-start(), calls=%async_computation.5 | async-start | bytes 1310720 | tf_op jit(solution)/shard_map/reduce_scatter | solution.py:105
  367.5 0.9 copy-start.8
  368.5 11.1 %collective-permute-start.6 = (f32[256,256]{1,0:T(8,128)S(1)}, f32[256,256]{1,0:T(8,128)S(1)}, u32[]{:S(2)}, u32[]{:S(2)}) collective-permute-start(f32[256,256]{1,0:T(8,128)S(1)} %get-tuple-element.234), channel_id=1, source_target_pairs={{0,1},{1,2},{2,3},{3,0},{4,5},{5,6},{6,7},{7,4},{8,9},{9,10},{10,1... | collective-permute-start | bytes 786440 | tf_op jit(solution)/shard_map/ppermute | solution.py:90
  370.1 13.9 %collective-permute-start.7 = (f32[256,256]{1,0:T(8,128)S(1)}, f32[256,256]{1,0:T(8,128)S(1)}, u32[]{:S(2)}, u32[]{:S(2)}) collective-permute-start(f32[256,256]{1,0:T(8,128)S(1)} %get-tuple-element.234), channel_id=1, source_target_pairs={{0,3},{1,0},{2,1},{3,2},{4,7},{5,4},{6,5},{7,6},{8,11},{9,8},{10,9... | collective-permute-start | bytes 786440 | tf_op jit(solution)/shard_map/ppermute | solution.py:95
  379.6 10.1 %collective-permute-start.8 = (f32[256,256]{1,0:T(8,128)S(1)}, f32[256,256]{1,0:T(8,128)S(1)}, u32[]{:S(2)}, u32[]{:S(2)}) collective-permute-start(f32[256,256]{1,0:T(8,128)S(1)} %collective-permute-done.6), channel_id=1, source_target_pairs={{0,1},{1,2},{2,3},{3,0},{4,5},{5,6},{6,7},{7,4},{8,9},{9,10},{10,1... | collective-permute-start | bytes 786440 | tf_op jit(solution)/shard_map/ppermute | solution.py:90
  423.0 1.0 copy-start
Sparse Core Ops, SparseCore 0:
  72.1 117.0 reduce-scatter.3
  245.8 121.5 reduce-scatter.5
  424.2 121.5 reduce-scatter.7
